TPU v7x, 32 devices: a whole 2x2x4 slice. The times are simulated.
32 devices in a mesh: gx: 8 (over z, core), gy: 4 (over y, x).
Axes of the slice: x: 2, y: 2, z: 4, core: 2. Of those that a mesh axis runs over, the one named last changes fastest.
Arguments:
- density: float32 [2, 128, 128, 128], P(None, 'gx', 'gy'), may hold values from 0.2 to 1
- cotangent: float32 [2, 128, 128, 128], P(None, 'gx', 'gy'), may hold values from -6 to 6
- adhesion: float32 [2, 2], replicated, may hold values from 1 to 3
Outputs:
- density_bar: float32 [2, 128, 128, 128], P(None, 'gx', 'gy')
All inputs are finite; a program needn't handle non-finite values.
Results may differ from a plain program's by a relative error of at most 0.000084.
Values sent between devices are 32-bit elements; how exact they have to be, the bound alone decides.
A program may use at most 64 MiB of HBM per device.

v0:
```python
import jax
import jax.numpy as jnp
from jax import lax
from jax.sharding import PartitionSpec as P

RADIUS = 16


time_step = 0.5
smoothing = 0.1
highest = lax.Precision.HIGHEST


def padded(cells, sides, width):
    for axis, dim in sides:
        count = lax.axis_size(axis)
        ends = count - 1
        head = lax.slice_in_dim(cells, 0, width, axis=dim)
        tail = lax.slice_in_dim(cells, cells.shape[dim] - width, cells.shape[dim], axis=dim)
        cells = jnp.concatenate(
            [
                lax.ppermute(tail, axis, [(i, (i + 1) % count) for i in range(ends)]),
                cells,
                lax.ppermute(head, axis, [((i + 1) % count, i) for i in range(ends)]),
            ],
            axis=dim,
        )
    return cells


def kernel_weight(offsets, antisym):
    magnitude = jnp.abs(offsets)
    weights = jnp.where(magnitude <= RADIUS, 1.0 - magnitude / (RADIUS + 1.0), 0.0)
    if antisym:
        weights = weights * offsets / RADIUS
    return weights


def kernel_norm(antisym):
    offsets = jnp.arange(-RADIUS, RADIUS + 1).astype(jnp.float32)
    weights = kernel_weight(offsets, antisym)
    return jnp.sqrt(jnp.sum(weights * weights))


def band_matrix(outputs, inputs, lead_in, antisym):
    row_index = lax.broadcasted_iota(jnp.int32, (outputs, inputs), 0)
    col_index = lax.broadcasted_iota(jnp.int32, (outputs, inputs), 1)
    offsets = (col_index - row_index - lead_in).astype(jnp.float32)
    return kernel_weight(offsets, antisym) / kernel_norm(antisym)


def along_x(matrix, values):
    return jnp.einsum("ck,fkyz->fcyz", matrix, values, precision=highest)


def along_y(matrix, values):
    return jnp.einsum("ck,fxkz->fxcz", matrix, values, precision=highest)


def along_z(matrix, values):
    return jnp.einsum("ck,fxyk->fxyc", matrix, values, precision=highest)


def face_terms(
    lower_density, upper_density, lower_cot, upper_cot, lower_velocity, upper_velocity, valid
):
    face_velocity = 0.5 * (lower_velocity + upper_velocity)
    magnitude = jnp.sqrt(face_velocity * face_velocity + smoothing * smoothing)
    flux_bar = jnp.where(valid, time_step * (upper_cot - lower_cot), 0.0)
    to_lower = flux_bar * 0.5 * (face_velocity + magnitude)
    to_upper = flux_bar * 0.5 * (face_velocity - magnitude)
    velocity_bar = flux_bar * (
        0.5 * (lower_density + upper_density)
        - 0.5 * face_velocity / magnitude * (upper_density - lower_density)
    )
    return (to_lower, to_upper, velocity_bar)


def raise_z(values):
    return jnp.concatenate([values[..., 1:], jnp.zeros_like(values[..., :1])], 3)


def drop_z(values):
    return jnp.concatenate([jnp.zeros_like(values[..., :1]), values[..., :-1]], 3)


def mix_fields(adhesion, fields):
    return (
        adhesion[:, 0, None, None, None] * fields[0][None]
        + adhesion[:, 1, None, None, None] * fields[1][None]
    )


def send_rims(density, cotangent, velocity_x, velocity_y):
    return padded(
        jnp.concatenate([density, cotangent, velocity_x, velocity_y], 0), (("gx", 1), ("gy", 2)), 1
    )


def body(density, cotangent, adhesion):
    cells_x = density.shape[1]
    cells_y = density.shape[2]
    cells_z = density.shape[3]
    wide_x = cells_x + 2 * RADIUS
    wide_y = cells_y + 2 * RADIUS
    even_x = band_matrix(cells_x, wide_x, RADIUS, False)
    odd_x = band_matrix(cells_x, wide_x, RADIUS, True)
    even_y = band_matrix(cells_y, wide_y, RADIUS, False)
    odd_y = band_matrix(cells_y, wide_y, RADIUS, True)
    even_z = band_matrix(cells_z, cells_z, 0, False)
    odd_z = band_matrix(cells_z, cells_z, 0, True)
    potential = mix_fields(adhesion, density)
    even_in_z = along_z(even_z, potential)
    odd_in_z = along_z(odd_z, potential)
    widened = padded(jnp.concatenate([even_in_z, odd_in_z], 0), (("gy", 2),), RADIUS)
    stacked = jnp.concatenate(
        [
            along_y(even_y, widened[0:2]),
            along_y(odd_y, widened[0:2]),
            along_y(even_y, widened[2:4]),
        ],
        0,
    )
    widened_x = padded(stacked, (("gx", 1),), RADIUS)
    velocity_x = along_x(odd_x, widened_x[0:2])
    velocity_y = along_x(even_x, widened_x[2:4])
    velocity_z = along_x(even_x, widened_x[4:6])
    rims = send_rims(density, cotangent, velocity_x, velocity_y)
    first_x = lax.axis_index("gx") * cells_x
    total_x = cells_x * lax.axis_size("gx")
    face_x = first_x - 1 + lax.broadcasted_iota(jnp.int32, (1, cells_x + 1, 1, 1), 1)
    valid_x = (face_x >= 0) & (face_x + 1 < total_x)
    strip_x = rims[:, :, 1 : cells_y + 1]
    lower_x = strip_x[:, 0 : cells_x + 1]
    upper_x = strip_x[:, 1 : cells_x + 2]
    to_lower, to_upper, velocity_bar = face_terms(
        lower_x[0:2], upper_x[0:2], lower_x[2:4], upper_x[2:4], lower_x[4:6], upper_x[4:6], valid_x
    )
    density_bar = to_lower[:, 1:] + to_upper[:, :cells_x]
    velocity_bar_x = 0.5 * (velocity_bar[:, 1:] + velocity_bar[:, :cells_x])
    first_y = lax.axis_index("gy") * cells_y
    total_y = cells_y * lax.axis_size("gy")
    face_y = first_y - 1 + lax.broadcasted_iota(jnp.int32, (1, 1, cells_y + 1, 1), 2)
    valid_y = (face_y >= 0) & (face_y + 1 < total_y)
    strip_y = rims[:, 1 : cells_x + 1]
    lower_y = strip_y[:, :, 0 : cells_y + 1]
    upper_y = strip_y[:, :, 1 : cells_y + 2]
    to_lower, to_upper, velocity_bar = face_terms(
        lower_y[0:2], upper_y[0:2], lower_y[2:4], upper_y[2:4], lower_y[6:8], upper_y[6:8], valid_y
    )
    density_bar = density_bar + to_lower[:, :, 1:] + to_upper[:, :, :cells_y]
    velocity_bar_y = 0.5 * (velocity_bar[:, :, 1:] + velocity_bar[:, :, :cells_y])
    face_z = lax.broadcasted_iota(jnp.int32, (1, 1, 1, cells_z), 3)
    valid_z = face_z + 1 < cells_z
    to_lower, to_upper, velocity_bar = face_terms(
        density,
        raise_z(density),
        cotangent,
        raise_z(cotangent),
        velocity_z,
        raise_z(velocity_z),
        valid_z,
    )
    density_bar = density_bar + to_lower + drop_z(to_upper)
    velocity_bar_z = 0.5 * (velocity_bar + drop_z(velocity_bar))
    spread_x = jnp.concatenate(
        [
            along_x(odd_x.T, velocity_bar_x),
            along_x(even_x.T, velocity_bar_y),
            along_x(even_x.T, velocity_bar_z),
        ],
        0,
    )
    margins_x = jnp.concatenate([spread_x[:, :RADIUS], spread_x[:, cells_x + RADIUS :]], 1)
    returned_x = padded(margins_x, (("gx", 1),), RADIUS)
    owned_x = (
        spread_x[:, RADIUS : cells_x + RADIUS]
        + returned_x[:, :RADIUS]
        + returned_x[:, 3 * RADIUS :]
    )
    spread_y = jnp.concatenate(
        [
            along_y(even_y.T, owned_x[0:2]) + along_y(odd_y.T, owned_x[2:4]),
            along_y(even_y.T, owned_x[4:6]),
        ],
        0,
    )
    margins_y = jnp.concatenate([spread_y[:, :, :RADIUS], spread_y[:, :, cells_y + RADIUS :]], 2)
    returned_y = padded(margins_y, (("gy", 2),), RADIUS)
    owned_y = (
        spread_y[:, :, RADIUS : cells_y + RADIUS]
        + jnp.pad(returned_y[:, :, :RADIUS], ((0, 0), (0, 0), (0, cells_y - RADIUS), (0, 0)))
        + jnp.pad(returned_y[:, :, 3 * RADIUS :], ((0, 0), (0, 0), (cells_y - RADIUS, 0), (0, 0)))
    )
    potential_bar = along_z(even_z.T, owned_y[0:2]) + along_z(odd_z.T, owned_y[2:4])
    return (
        cotangent
        + density_bar
        + adhesion[0, :, None, None, None] * potential_bar[0][None]
        + adhesion[1, :, None, None, None] * potential_bar[1][None]
    )


def solution(mesh):
    return jax.shard_map(
        body,
        mesh=mesh,
        in_specs=(P(None, "gx", "gy", None), P(None, "gx", "gy", None), P()),
        out_specs=P(None, "gx", "gy", None),
        check_vma=False,
    )
```

profile of v0, /device:TPU:17, one launch (start us, length us, event | category | flops | bytes accessed | tf_op | source)
XLA Modules:
  0.0 154.0 jit_solution(3725391719031831972)
XLA Ops:
  0.0 0.6 multiply_reduce_fusion.1
  0.6 0.6 multiply_reduce_fusion
  1.9 1.1 slice_bitcast_fusion.3
  3.0 1.0 slice_reduce_fusion.1
  4.6 0.6 fusion.48
  5.2 0.6 fusion.47
  5.9 3.1 %collective-permute-start = (f32[4,16,16,128]{3,2,1,0:T(8,128)S(1)}, f32[4,16,16,128]{3,2,1,0:T(8,128)S(1)}, u32[]{:S(2)}, u32[]{:S(2)}) collective-permute-start(f32[4,16,16,128]{3,2,1,0:T(8,128)S(1)} %get-tuple-element.26), channel_id=1, source_target_pairs={{0,1},{1,2},{2,3},{4,5},{5,6},{6,7},{8,9},{9,10},{10,11},{12,13},{... | collective-permute-start | bytes 1572872 | tf_op jit(solution)/shard_map/ppermute | solution.py:22
  9.1 1.3 collective-permute-start.1
  10.4 9.2 %collective-permute-done = f32[4,16,16,128]{3,2,1,0:T(8,128)S(1)} collective-permute-done((f32[4,16,16,128]{3,2,1,0:T(8,128)S(1)}, f32[4,16,16,128]{3,2,1,0:T(8,128)S(1)}, u32[]{:S(2)}, u32[]{:S(2)}) %collective-permute-start) | collective-permute-done | bytes 524320 | tf_op jit(solution)/shard_map/ppermute | solution.py:22
  19.6 13.2 %collective-permute-done.1 = f32[4,16,16,128]{3,2,1,0:T(8,128)S(1)} collective-permute-done((f32[4,16,16,128]{3,2,1,0:T(8,128)S(1)}, f32[4,16,16,128]{3,2,1,0:T(8,128)S(1)}, u32[]{:S(2)}, u32[]{:S(2)}) %collective-permute-start.1) | collective-permute-done | bytes 524320 | tf_op jit(solution)/shard_map/ppermute | solution.py:24
  32.8 0.7 convolution_bitcast_fusion.6
  33.5 0.7 convolution_bitcast_fusion.4
  34.2 0.7 convolution_bitcast_fusion.5
  35.0 1.3 pad_maximum_fusion.3
  36.3 4.6 %collective-permute-start.2 = (f32[6,16,32,128]{3,2,1,0:T(8,128)}, f32[6,16,32,128]{3,2,1,0:T(8,128)}, u32[]{:S(2)}, u32[]{:S(2)}) collective-permute-start(f32[6,16,32,128]{3,2,1,0:T(8,128)} %pad_maximum_fusion.3), channel_id=1, source_target_pairs={{0,4},{4,8},{8,12},{12,16},{16,20},{20,24},{24,28},{1,5},{5,9},{9,... | collective-permute-start | bytes 4718600 | tf_op jit(solution)/shard_map/ppermute | solution.py:22
  41.0 1.9 %collective-permute-start.3 = (f32[6,16,32,128]{3,2,1,0:T(8,128)}, f32[6,16,32,128]{3,2,1,0:T(8,128)}, u32[]{:S(2)}, u32[]{:S(2)}) collective-permute-start(f32[6,16,32,128]{3,2,1,0:T(8,128)} %pad_maximum_fusion.3), channel_id=1, source_target_pairs={{4,0},{8,4},{12,8},{16,12},{20,16},{24,20},{28,24},{5,1},{9,5},{13... | collective-permute-start | bytes 4718600 | tf_op jit(solution)/shard_map/ppermute | solution.py:24
  44.0 14.6 %collective-permute-done.2 = f32[6,16,32,128]{3,2,1,0:T(8,128)} collective-permute-done((f32[6,16,32,128]{3,2,1,0:T(8,128)}, f32[6,16,32,128]{3,2,1,0:T(8,128)}, u32[]{:S(2)}, u32[]{:S(2)}) %collective-permute-start.2) | collective-permute-done | bytes 1572896 | tf_op jit(solution)/shard_map/ppermute | solution.py:22
  58.6 4.4 %collective-permute-done.3 = f32[6,16,32,128]{3,2,1,0:T(8,128)} collective-permute-done((f32[6,16,32,128]{3,2,1,0:T(8,128)}, f32[6,16,32,128]{3,2,1,0:T(8,128)}, u32[]{:S(2)}, u32[]{:S(2)}) %collective-permute-start.3) | collective-permute-done | bytes 1572896 | tf_op jit(solution)/shard_map/ppermute | solution.py:24
  63.0 2.7 %pad_maximum_fusion = f32[6,48,32,128]{3,2,1,0:T(8,128)S(1)} fusion(f32[6,16,32,128]{3,2,1,0:T(8,128)} %collective-permute-done.3, f32[2,16,32,128]{3,2,1,0:T(8,128)} %copy-done.3, f32[2,16,32,128]{3,2,1,0:T(8,128)} %copy-done.4, f32[2,16,32,128]{3,2,1,0:T(8,128)} %copy-done.2, f32[6,16,32,128]{3,2,1,0:T(8,128)} %collective-permute-done.2), kind=kLoop, calls=%fused_computation | loop fusion | flops 4718592 | bytes 9437184 | tf_op jit(solution)/shard_map/concatenate | solution.py:20
  65.7 1.0 fusion.194
  66.7 1.8 %fusion.8 = f32[2,16,32,128]{3,1,2,0:T(8,128)S(1)} fusion(f32[2,48,32,128]{3,2,1,0:T(8,128)S(1)} %get-tuple-element.15, f32[]{:T(128)S(6)} %sqrt.20), kind=kOutput, calls=%fused_computation.22 | convolution fusion | flops 75505920 | bytes 2097156 | tf_op jit(solution)/shard_map/ck,fkyz->fcyz/dot_general | solution.py:53
  68.6 1.8 %fusion.11 = f32[2,16,32,128]{3,1,2,0:T(8,128)S(1)} fusion(f32[2,48,32,128]{3,2,1,0:T(8,128)S(1)} %get-tuple-element.14, f32[]{:T(128)S(6)} %sqrt.19), kind=kOutput, calls=%fused_computation.23 | convolution fusion | flops 75504384 | bytes 2097156 | tf_op jit(solution)/shard_map/ck,fkyz->fcyz/dot_general | solution.py:53
  70.6 1.9 %collective-permute-start.4 = (f32[8,1,32,128]{3,1,2,0:T(1,128)S(1)}, f32[8,1,32,128]{3,1,2,0:T(1,128)S(1)}, u32[]{:S(2)}, u32[]{:S(2)}) collective-permute-start(f32[8,1,32,128]{3,1,2,0:T(1,128)S(1)} %get-tuple-element.21), channel_id=1, source_target_pairs={{4,0},{8,4},{12,8},{16,12},{20,16},{24,20},{28,24},{5,1},{9,5},{13... | collective-permute-start | bytes 393224 | tf_op jit(solution)/shard_map/ppermute | solution.py:24
  72.5 3.8 %collective-permute-start.5 = (f32[8,1,32,128]{3,1,2,0:T(1,128)S(1)}, f32[8,1,32,128]{3,1,2,0:T(1,128)S(1)}, u32[]{:S(2)}, u32[]{:S(2)}) collective-permute-start(f32[8,1,32,128]{3,1,2,0:T(1,128)S(1)} %get-tuple-element.20), channel_id=1, source_target_pairs={{0,4},{4,8},{8,12},{12,16},{16,20},{20,24},{24,28},{1,5},{5,9},{9,... | collective-permute-start | bytes 393224 | tf_op jit(solution)/shard_map/ppermute | solution.py:22
  76.4 1.8 %fusion.14 = f32[2,16,32,128]{3,1,2,0:T(8,128)S(1)} fusion(f32[2,48,32,128]{3,2,1,0:T(8,128)S(1)} %get-tuple-element.13, f32[]{:T(128)S(6)} %sqrt.19), kind=kOutput, calls=%fused_computation.24 | convolution fusion | flops 75504384 | bytes 2097156 | tf_op jit(solution)/shard_map/ck,fkyz->fcyz/dot_general | solution.py:53
  78.4 0.9 subtract_multiply_fusion.2
  79.3 1.5 convolution_bitcast_fusion
  80.8 1.3 collective-permute-start.6
  82.1 4.0 %collective-permute-start.7 = (f32[8,18,1,128]{3,1,2,0:T(8,128)S(1)}, f32[8,18,1,128]{3,1,2,0:T(8,128)S(1)}, u32[]{:S(2)}, u32[]{:S(2)}) collective-permute-start(f32[8,18,1,128]{3,1,2,0:T(8,128)S(1)} %get-tuple-element.17), channel_id=1, source_target_pairs={{0,1},{1,2},{2,3},{4,5},{5,6},{6,7},{8,9},{9,10},{10,11},{12,13},{... | collective-permute-start | bytes 221192 | tf_op jit(solution)/shard_map/ppermute | solution.py:22
  86.1 2.3 %subtract_multiply_fusion = f32[2,17,32,128]{3,1,2,0:T(8,128)S(1)} fusion(f32[2,16,32,128]{3,1,2,0:T(8,128)S(1)} %fusion.11, f32[2,16,32,128]{3,1,2,0:T(8,128)S(1)} %fusion.8, f32[2,16,32,128]{3,1,2,0:T(8,128)S(1)} %copy.11, f32[2,16,32,128]{3,1,2,0:T(8,128)S(1)} %copy.6, f32[8,1,32,128]{3,1,2,0:T(1,128)S(1)} %collective-permute-done.5, ...), kind=kLoop, calls=%fused_computation.46 | loop fusion | flops 5431296 | bytes 2916369 | tf_op jit(solution)/shard_map/mul | solution.py:72
  88.4 1.4 convolution_bitcast_fusion.2
  89.9 1.4 subtract_multiply_fusion.1
  91.4 1.4 convolution_bitcast_fusion.1
  93.6 2.5 %collective-permute-start.8 = (f32[6,16,32,128]{3,1,2,0:T(8,128)S(1)}, f32[6,16,32,128]{3,1,2,0:T(8,128)S(1)}, u32[]{:S(2)}, u32[]{:S(2)}) collective-permute-start(f32[6,16,32,128]{3,1,2,0:T(8,128)S(1)} %get-tuple-element.11), channel_id=1, source_target_pairs={{0,4},{4,8},{8,12},{12,16},{16,20},{20,24},{24,28},{1,5},{5,9},{9,... | collective-permute-start | bytes 4718600 | tf_op jit(solution)/shard_map/ppermute | solution.py:22
  96.1 2.1 %collective-permute-start.9 = (f32[6,16,32,128]{3,1,2,0:T(8,128)S(1)}, f32[6,16,32,128]{3,1,2,0:T(8,128)S(1)}, u32[]{:S(2)}, u32[]{:S(2)}) collective-permute-start(f32[6,16,32,128]{3,1,2,0:T(8,128)S(1)} %get-tuple-element.12), channel_id=1, source_target_pairs={{4,0},{8,4},{12,8},{16,12},{20,16},{24,20},{28,24},{5,1},{9,5},{13... | collective-permute-start | bytes 4718600 | tf_op jit(solution)/shard_map/ppermute | solution.py:24
  98.9 14.5 %collective-permute-done.8 = f32[6,16,32,128]{3,1,2,0:T(8,128)S(1)} collective-permute-done((f32[6,16,32,128]{3,1,2,0:T(8,128)S(1)}, f32[6,16,32,128]{3,1,2,0:T(8,128)S(1)}, u32[]{:S(2)}, u32[]{:S(2)}) %collective-permute-start.8) | collective-permute-done | bytes 1572896 | tf_op jit(solution)/shard_map/ppermute | solution.py:22
  113.4 4.4 %collective-permute-done.9 = f32[6,16,32,128]{3,1,2,0:T(8,128)S(1)} collective-permute-done((f32[6,16,32,128]{3,1,2,0:T(8,128)S(1)}, f32[6,16,32,128]{3,1,2,0:T(8,128)S(1)}, u32[]{:S(2)}, u32[]{:S(2)}) %collective-permute-start.9) | collective-permute-done | bytes 1572896 | tf_op jit(solution)/shard_map/ppermute | solution.py:24
  118.3 1.1 fusion.41
  119.4 1.1 convolution_bitcast_fusion.3
  120.6 1.1 fusion.7
  121.7 4.0 %collective-permute-start.10 = (f32[4,16,16,128]{3,2,1,0:T(8,128)S(1)}, f32[4,16,16,128]{3,2,1,0:T(8,128)S(1)}, u32[]{:S(2)}, u32[]{:S(2)}) collective-permute-start(f32[4,16,16,128]{3,2,1,0:T(8,128)S(1)} %get-tuple-element.18), channel_id=1, source_target_pairs={{0,1},{1,2},{2,3},{4,5},{5,6},{6,7},{8,9},{9,10},{10,11},{12,13},{... | collective-permute-start | bytes 1572872 | tf_op jit(solution)/shard_map/ppermute | solution.py:22
  125.8 1.3 collective-permute-start.11
  127.8 8.8 %collective-permute-done.10 = f32[4,16,16,128]{3,2,1,0:T(8,128)S(1)} collective-permute-done((f32[4,16,16,128]{3,2,1,0:T(8,128)S(1)}, f32[4,16,16,128]{3,2,1,0:T(8,128)S(1)}, u32[]{:S(2)}, u32[]{:S(2)}) %collective-permute-start.10) | collective-permute-done | bytes 524320 | tf_op jit(solution)/shard_map/ppermute | solution.py:22
  136.6 13.9 %collective-permute-done.11 = f32[4,16,16,128]{3,2,1,0:T(8,128)S(1)} collective-permute-done((f32[4,16,16,128]{3,2,1,0:T(8,128)S(1)}, f32[4,16,16,128]{3,2,1,0:T(8,128)S(1)}, u32[]{:S(2)}, u32[]{:S(2)}) %collective-permute-start.11) | collective-permute-done | bytes 524320 | tf_op jit(solution)/shard_map/ppermute | solution.py:24
  150.5 0.6 fusion.60
  151.1 0.6 convolution_add_fusion.1
  152.0 1.0 fusion.37
  153.0 1.0 copy.20
  (43 shorter events, 4.6 us)
Async XLA Ops:
  5.9 13.7 %collective-permute-start = (f32[4,16,16,128]{3,2,1,0:T(8,128)S(1)}, f32[4,16,16,128]{3,2,1,0:T(8,128)S(1)}, u32[]{:S(2)}, u32[]{:S(2)}) collective-permute-start(f32[4,16,16,128]{3,2,1,0:T(8,128)S(1)} %get-tuple-element.26), channel_id=1, source_target_pairs={{0,1},{1,2},{2,3},{4,5},{5,6},{6,7},{8,9},{9,10},{10,11},{12,13},{... | collective-permute-start | bytes 1572872 | tf_op jit(solution)/shard_map/ppermute | solution.py:22
  9.1 23.7 %collective-permute-start.1 = (f32[4,16,16,128]{3,2,1,0:T(8,128)S(1)}, f32[4,16,16,128]{3,2,1,0:T(8,128)S(1)}, u32[]{:S(2)}, u32[]{:S(2)}) collective-permute-start(f32[4,16,16,128]{3,2,1,0:T(8,128)S(1)} %get-tuple-element.27), channel_id=1, source_target_pairs={{1,0},{2,1},{3,2},{5,4},{6,5},{7,6},{9,8},{10,9},{11,10},{13,12},{... | collective-permute-start | bytes 1572872 | tf_op jit(solution)/shard_map/ppermute | solution.py:24
  33.5 1.4 copy-start.2
  34.2 2.1 %copy-start.3 = (f32[2,16,32,128]{3,2,1,0:T(8,128)}, f32[2,16,32,128]{3,2,1,0:T(8,128)S(1)}, u32[]{:S(2)}) copy-start(f32[2,16,32,128]{3,2,1,0:T(8,128)S(1)} %convolution_bitcast_fusion.4) | copy-start | bytes 1572868
  35.0 1.4 copy-start.4
  35.0 7.9 %copy-start.1 = (f32[2,16,32,128]{3,2,1,0:T(8,128)S(1)}, f32[2,16,32,128]{3,2,1,0:T(8,128)}, u32[]{:S(2)}) copy-start(f32[2,16,32,128]{3,2,1,0:T(8,128)} %param.3) | copy-start | bytes 1572868
  35.0 8.2 %copy-start = (f32[2,16,32,128]{3,2,1,0:T(8,128)S(1)}, f32[2,16,32,128]{3,2,1,0:T(8,128)}, u32[]{:S(2)}) copy-start(f32[2,16,32,128]{3,2,1,0:T(8,128)} %param.4) | copy-start | bytes 1572868
  36.3 22.3 %collective-permute-start.2 = (f32[6,16,32,128]{3,2,1,0:T(8,128)}, f32[6,16,32,128]{3,2,1,0:T(8,128)}, u32[]{:S(2)}, u32[]{:S(2)}) collective-permute-start(f32[6,16,32,128]{3,2,1,0:T(8,128)} %pad_maximum_fusion.3), channel_id=1, source_target_pairs={{0,4},{4,8},{8,12},{12,16},{16,20},{20,24},{24,28},{1,5},{5,9},{9,... | collective-permute-start | bytes 4718600 | tf_op jit(solution)/shard_map/ppermute | solution.py:22
  41.0 22.1 %collective-permute-start.3 = (f32[6,16,32,128]{3,2,1,0:T(8,128)}, f32[6,16,32,128]{3,2,1,0:T(8,128)}, u32[]{:S(2)}, u32[]{:S(2)}) collective-permute-start(f32[6,16,32,128]{3,2,1,0:T(8,128)} %pad_maximum_fusion.3), channel_id=1, source_target_pairs={{4,0},{8,4},{12,8},{16,12},{20,16},{24,20},{28,24},{5,1},{9,5},{13... | collective-permute-start | bytes 4718600 | tf_op jit(solution)/shard_map/ppermute | solution.py:24
  70.6 10.2 %collective-permute-start.4 = (f32[8,1,32,128]{3,1,2,0:T(1,128)S(1)}, f32[8,1,32,128]{3,1,2,0:T(1,128)S(1)}, u32[]{:S(2)}, u32[]{:S(2)}) collective-permute-start(f32[8,1,32,128]{3,1,2,0:T(1,128)S(1)} %get-tuple-element.21), channel_id=1, source_target_pairs={{4,0},{8,4},{12,8},{16,12},{20,16},{24,20},{28,24},{5,1},{9,5},{13... | collective-permute-start | bytes 393224 | tf_op jit(solution)/shard_map/ppermute | solution.py:24
  72.5 8.2 %collective-permute-start.5 = (f32[8,1,32,128]{3,1,2,0:T(1,128)S(1)}, f32[8,1,32,128]{3,1,2,0:T(1,128)S(1)}, u32[]{:S(2)}, u32[]{:S(2)}) collective-permute-start(f32[8,1,32,128]{3,1,2,0:T(1,128)S(1)} %get-tuple-element.20), channel_id=1, source_target_pairs={{0,4},{4,8},{8,12},{12,16},{16,20},{20,24},{24,28},{1,5},{5,9},{9,... | collective-permute-start | bytes 393224 | tf_op jit(solution)/shard_map/ppermute | solution.py:22
  80.8 9.1 %collective-permute-start.6 = (f32[8,18,1,128]{3,1,2,0:T(8,128)S(1)}, f32[8,18,1,128]{3,1,2,0:T(8,128)S(1)}, u32[]{:S(2)}, u32[]{:S(2)}) collective-permute-start(f32[8,18,1,128]{3,1,2,0:T(8,128)S(1)} %get-tuple-element.16), channel_id=1, source_target_pairs={{1,0},{2,1},{3,2},{5,4},{6,5},{7,6},{9,8},{10,9},{11,10},{13,12},{... | collective-permute-start | bytes 221192 | tf_op jit(solution)/shard_map/ppermute | solution.py:24
  82.1 7.8 %collective-permute-start.7 = (f32[8,18,1,128]{3,1,2,0:T(8,128)S(1)}, f32[8,18,1,128]{3,1,2,0:T(8,128)S(1)}, u32[]{:S(2)}, u32[]{:S(2)}) collective-permute-start(f32[8,18,1,128]{3,1,2,0:T(8,128)S(1)} %get-tuple-element.17), channel_id=1, source_target_pairs={{0,1},{1,2},{2,3},{4,5},{5,6},{6,7},{8,9},{9,10},{10,11},{12,13},{... | collective-permute-start | bytes 221192 | tf_op jit(solution)/shard_map/ppermute | solution.py:22
  93.4 4.9 %copy-start.5 = (f32[2,2]{1,0:T(2,128)S(1)}, f32[2,2]{1,0:T(2,128)}, u32[]{:S(2)}) copy-start(f32[2,2]{1,0:T(2,128)} %param.5) | copy-start | bytes 52
  93.6 19.8 %collective-permute-start.8 = (f32[6,16,32,128]{3,1,2,0:T(8,128)S(1)}, f32[6,16,32,128]{3,1,2,0:T(8,128)S(1)}, u32[]{:S(2)}, u32[]{:S(2)}) collective-permute-start(f32[6,16,32,128]{3,1,2,0:T(8,128)S(1)} %get-tuple-element.11), channel_id=1, source_target_pairs={{0,4},{4,8},{8,12},{12,16},{16,20},{20,24},{24,28},{1,5},{5,9},{9,... | collective-permute-start | bytes 4718600 | tf_op jit(solution)/shard_map/ppermute | solution.py:22
  96.1 21.7 %collective-permute-start.9 = (f32[6,16,32,128]{3,1,2,0:T(8,128)S(1)}, f32[6,16,32,128]{3,1,2,0:T(8,128)S(1)}, u32[]{:S(2)}, u32[]{:S(2)}) collective-permute-start(f32[6,16,32,128]{3,1,2,0:T(8,128)S(1)} %get-tuple-element.12), channel_id=1, source_target_pairs={{4,0},{8,4},{12,8},{16,12},{20,16},{24,20},{28,24},{5,1},{9,5},{13... | collective-permute-start | bytes 4718600 | tf_op jit(solution)/shard_map/ppermute | solution.py:24
  121.7 14.8 %collective-permute-start.10 = (f32[4,16,16,128]{3,2,1,0:T(8,128)S(1)}, f32[4,16,16,128]{3,2,1,0:T(8,128)S(1)}, u32[]{:S(2)}, u32[]{:S(2)}) collective-permute-start(f32[4,16,16,128]{3,2,1,0:T(8,128)S(1)} %get-tuple-element.18), channel_id=1, source_target_pairs={{0,1},{1,2},{2,3},{4,5},{5,6},{6,7},{8,9},{9,10},{10,11},{12,13},{... | collective-permute-start | bytes 1572872 | tf_op jit(solution)/shard_map/ppermute | solution.py:22
  125.8 24.7 %collective-permute-start.11 = (f32[4,16,16,128]{3,2,1,0:T(8,128)S(1)}, f32[4,16,16,128]{3,2,1,0:T(8,128)S(1)}, u32[]{:S(2)}, u32[]{:S(2)}) collective-permute-start(f32[4,16,16,128]{3,2,1,0:T(8,128)S(1)} %get-tuple-element.19), channel_id=1, source_target_pairs={{1,0},{2,1},{3,2},{5,4},{6,5},{7,6},{9,8},{10,9},{11,10},{13,12},{... | collective-permute-start | bytes 1572872 | tf_op jit(solution)/shard_map/ppermute | solution.py:24
where the time goes:
time: 154 us
  waiting for transfers between devices  83.1 us (54%)
  starting transfers between devices  32 us (21%)
  matrix products  17.6 us (11%)
  other arithmetic  13.6 us (9%)
  local copies, waits for them, and re-layouts  5.91 us (4%)
  between operations  1.86 us (1%)
    ppermute x6, waiting for transfers between devices, padded(): lax.ppermute(tail, axis, [(i, (i + 1) % count) for i in range(ends)])  47.2 us
    ppermute x6, waiting for transfers between devices, padded(): lax.ppermute(head, axis, [((i + 1) % count, i) for i in range(ends)])  35.9 us
    ppermute x6, starting transfers between devices, padded(): lax.ppermute(tail, axis, [(i, (i + 1) % count) for i in range(ends)])  22.1 us
    ppermute x6, starting transfers between devices, padded(): lax.ppermute(head, axis, [((i + 1) % count, i) for i in range(ends)])  9.86 us
    dot_general x6, matrix products, along_x(): return jnp.einsum('ck,fkyz->fcyz', matrix, values, precision=highest)  9.79 us
    dot_general x6, matrix products, along_y(): return jnp.einsum('ck,fxkz->fxcz', matrix, values, precision=highest)  5.38 us
    mul x3, other arithmetic, face_terms(): flux_bar * (0.5 * (lower_density + upper_density) - 0.5 * face_velocity /...  4.63 us
  transfers between devices with their start and end apart: 12, of which 8 were waited for; matrix products, arithmetic and copies ran while one was open for 7% of the time, Pallas kernels for 0%

commit v1 on v0

v1 whole, which is shorter than its diff:
```python
import math

import jax
import jax.numpy as jnp
from jax import lax
from jax.experimental import pallas as pl
from jax.experimental.pallas import tpu as pltpu
from jax.sharding import PartitionSpec as P

R = 16
TIME_STEP = 0.5
SMOOTHING = 0.1
MESH = pl.DeviceIdType.MESH
F32 = jnp.float32
BF16 = jnp.bfloat16


def even_int(d):
    return jnp.maximum(R + 1.0 - jnp.abs(d), 0.0)


def odd_int(d):
    return even_int(d) * d


def weight_scale():
    e = sum((R + 1 - abs(d)) ** 2 for d in range(-R, R + 1))
    o = sum(((R + 1 - abs(d)) * d) ** 2 for d in range(-R, R + 1))
    return 1.0 / (math.sqrt(o) * e)


def offsets(rows, cols, lead):
    r = lax.broadcasted_iota(jnp.int32, (rows, cols), 0)
    c = lax.broadcasted_iota(jnp.int32, (rows, cols), 1)
    return (c - r - lead).astype(F32)


def split(v):
    hi = v.astype(BF16)
    return hi, (v - hi.astype(F32)).astype(BF16)


def dot(a, b):
    return lax.dot_general(a, b, (((1,), (0,)), ((), ())), preferred_element_type=F32)


def filter_rows(p, count):
    def box(k):
        s = p[k]
        for j in range(k + 1, k + R + 1):
            s = s + p[j]
        return s

    def start_odd(c):
        s = None
        for d in range(1, R + 1):
            t = float((R + 1 - d) * d) * (p[c + R + d] - p[c + R - d])
            s = t if s is None else s + t
        return s

    e0 = float(R + 1) * p[R]
    for d in range(1, R + 1):
        e0 = e0 + float(R + 1 - d) * (p[R + d] + p[R - d])
    even, odd = [e0], [start_odd(0), start_odd(1)]
    slope = odd[1] - odd[0]
    lo, hi = box(0), box(R + 1)
    for c in range(count - 1):
        if c > 0:
            lo = lo + (p[c + R] - p[c - 1])
            hi = hi + (p[c + 2 * R + 1] - p[c + R])
        delta = hi - lo
        even.append(even[-1] + delta)
        if c > 0:
            slope = slope + (
                (R + 2.0) * p[c + 2 * R + 1] - 2.0 * (delta + p[c + R]) - float(R) * p[c - 1]
            )
            odd.append(odd[-1] + slope)
    return even, odd


def spread_rows(q, p):
    n = len(q)

    def prefix(v):
        c = [None, v[0]]
        for k in range(1, n):
            c.append(c[-1] + v[k])
        return c

    cq, cp = prefix(q), prefix(p)

    def at(c, k):
        return c[min(max(k, 0), n)]

    def total(terms):
        s = None
        for w, v in terms:
            if v is None or w == 0.0:
                continue
            t = v if w == 1.0 else w * v
            s = t if s is None else s + t
        return s

    def plus(a, b):
        if a is None:
            return b
        return a if b is None else a + b

    out, slope, value = [], None, None
    for j in range(-1, n + 2 * R - 1):
        inner = [(1.0, at(cp, j + 1)), (-1.0, at(cp, j - R + 1)), (-1.0, at(cp, j - R)), (1.0, at(cp, j - 2 * R))]
        terms = {}
        for w, v in inner:
            if v is not None:
                terms[id(v)] = (terms.get(id(v), (0.0, v))[0] + 2.0 * w, v)
        terms = list(terms.values())
        if 0 <= j - 2 * R - 1 < n:
            terms.append((float(R), p[j - 2 * R - 1]))
        if 0 <= j + 1 < n:
            terms.append((-float(R), p[j + 1]))
        slope = plus(slope, total(terms))
        terms = {}
        for w, v in [(1.0, at(cq, j + 2)), (-2.0, at(cq, j - R + 1)), (1.0, at(cq, j - 2 * R))]:
            if v is not None:
                terms[id(v)] = (terms.get(id(v), (0.0, v))[0] + w, v)
        value = plus(value, plus(slope, total(list(terms.values()))))
        out.append(value)
    return out


def face_terms(lower_d, upper_d, lower_c, upper_c, lower_v, upper_v, valid):
    f = 0.5 * (lower_v + upper_v)
    square = f * f + SMOOTHING * SMOOTHING
    inverse = lax.rsqrt(square)
    magnitude = square * inverse
    bar = jnp.where(valid, (0.5 * TIME_STEP) * (upper_c - lower_c), 0.0)
    return (
        bar * (f + magnitude),
        bar * (f - magnitude),
        bar * ((lower_d + upper_d) - (f * inverse) * (upper_d - lower_d)),
    )


class Pair:
    def __init__(self, axis, place, src_up, dst_up, src_down, dst_down, send, recv, index, only=None):
        self.lo, self.hi = place["has_lo"], place["has_hi"]
        if only is not None:
            self.lo, self.hi = self.lo & only, self.hi & only
        self.up = pltpu.make_async_remote_copy(
            src_ref=src_up, dst_ref=dst_up, send_sem=send.at[index], recv_sem=recv.at[index],
            device_id={axis: place["hi"]}, device_id_type=MESH)
        self.down = pltpu.make_async_remote_copy(
            src_ref=src_down, dst_ref=dst_down, send_sem=send.at[index + 1], recv_sem=recv.at[index + 1],
            device_id={axis: place["lo"]}, device_id_type=MESH)

    def start(self):
        pl.when(self.hi)(lambda: self.up.start())
        pl.when(self.lo)(lambda: self.down.start())

    def wait_recv(self):
        pl.when(self.lo)(lambda: self.up.wait_recv())
        pl.when(self.hi)(lambda: self.down.wait_recv())

    def wait_send(self):
        pl.when(self.hi)(lambda: self.up.wait_send())
        pl.when(self.lo)(lambda: self.down.wait_send())


def place_on(axis, count):
    me = lax.axis_index(axis)
    return {
        "has_lo": me > 0,
        "has_hi": me < count - 1,
        "lo": jnp.maximum(me - 1, 0),
        "hi": jnp.minimum(me + 1, count - 1),
    }


def kernel(nx, ny, adh, den, cot, out, pot, uv, tri, vx, vyz, zt, dcx, rim_y, stage_y, rim_vy, stage_vy,
           spread, rx, ry, wy, wyt, wz, send, recv):
    X, Y, Z = den.shape[1:]
    XE, YE = X + 2 * R, Y + 2 * R
    gx, gy = place_on("gx", nx), place_on("gy", ny)
    scale = weight_scale()

    barrier = pltpu.get_barrier_semaphore()
    for axis, place in (("gx", gx), ("gy", gy)):
        for has, other in ((place["has_lo"], place["lo"]), (place["has_hi"], place["hi"])):
            @pl.when(has)
            def _():
                pl.semaphore_signal(barrier, inc=1, device_id={axis: other}, device_id_type=MESH)

    def zero(ref):
        ref[...] = jnp.zeros(ref.shape, ref.dtype)

    @pl.when(jnp.logical_not(gx["has_lo"]))
    def _():
        zero(pot.at[:, 0:R])
        zero(rx.at[:, 0])
        zero(dcx.at[:, 0:1])
        zero(vx.at[:, 0:1])

    @pl.when(jnp.logical_not(gx["has_hi"]))
    def _():
        zero(pot.at[:, R + X:])
        zero(rx.at[:, 1])
        zero(dcx.at[:, X + 1:])
        zero(vx.at[:, X + 1:])

    @pl.when(jnp.logical_not(gy["has_lo"]))
    def _():
        zero(pot.at[:, :, 0:R])
        zero(ry.at[:, 0])
        zero(rim_y.at[0])
        zero(rim_vy.at[:, 0])

    @pl.when(jnp.logical_not(gy["has_hi"]))
    def _():
        zero(pot.at[:, :, R + Y:])
        zero(ry.at[:, 1])
        zero(rim_y.at[1])
        zero(rim_vy.at[:, 1])

    a = [[adh[i, j] * scale for j in range(2)] for i in range(2)]

    def mix(x, carry):
        d = [den[0, x], den[1, x]]
        for i in range(2):
            pot[i, R + x, R:R + Y, :] = a[i][0] * d[0] + a[i][1] * d[1]
            dcx[i, 1 + x] = d[i]
            dcx[2 + i, 1 + x] = cot[i, x]
        return carry

    lax.fori_loop(0, X, mix, 0)
    for i in range(2):
        for x in range(X):
            stage_y[0, i, x:x + 1, :] = den[i, x, 0:1, :]
            stage_y[1, i, x:x + 1, :] = den[i, x, Y - 1:Y, :]
            stage_y[0, 2 + i, x:x + 1, :] = cot[i, x, 0:1, :]
            stage_y[1, 2 + i, x:x + 1, :] = cot[i, x, Y - 1:Y, :]

    peers = sum(place[has].astype(jnp.int32) for place in (gx, gy) for has in ("has_lo", "has_hi"))
    pl.semaphore_wait(barrier, peers)

    cx, cy = slice(R, R + X), slice(R, R + Y)
    sends = []
    counter = [0]

    def pair(axis, *refs, only=None):
        index = counter[0]
        counter[0] += 2
        made = Pair(axis, gx if axis == "gx" else gy, *refs, send, recv, index, only)
        sends.append(made)
        return made

    to_y, to_x = [], []
    for i in range(2):
        to_y.append(pair("gy", pot.at[i, cx, Y:Y + R], pot.at[i, cx, 0:R],
                         pot.at[i, cx, R:2 * R], pot.at[i, cx, R + Y:YE]))
        to_x.append(pair("gx", pot.at[i, X:X + R, cy], pot.at[i, 0:R, cy],
                         pot.at[i, R:2 * R, cy], pot.at[i, R + X:XE, cy]))
        to_y[i].start()
        to_x[i].start()
    rims = [
        pair("gx", dcx.at[:, X], dcx.at[:, 0], dcx.at[:, 1], dcx.at[:, X + 1]),
        pair("gy", stage_y.at[1], rim_y.at[0], stage_y.at[0], rim_y.at[1]),
    ]

    o = offsets(Y, YE, R)
    for k in range(2):
        wy[0:Y, k * YE:(k + 1) * YE] = even_int(o).astype(BF16)
        wy[Y:2 * Y, k * YE:(k + 1) * YE] = odd_int(o).astype(BF16)
    o = -offsets(YE, Y, -R)
    for k in range(2):
        wyt[:, k * Y:(k + 1) * Y] = even_int(o).astype(BF16)
        wyt[:, (2 + k) * Y:(3 + k) * Y] = odd_int(o).astype(BF16)
    o = offsets(Z, Z, 0)
    for k in range(2):
        wz[0, k * Z:(k + 1) * Z, :] = even_int(o).astype(BF16)
        wz[1, k * Z:(k + 1) * Z, :] = odd_int(-o).astype(BF16)
        wz[2, k * Z:(k + 1) * Z, :] = odd_int(o).astype(BF16)

    corners = []
    for i in range(2):
        to_y[i].wait_recv()
        made = []
        for part, only in ((slice(0, R), gy["has_lo"]), (slice(R + Y, YE), gy["has_hi"])):
            made.append(pair("gx", pot.at[i, X:X + R, part], pot.at[i, 0:R, part],
                             pot.at[i, R:2 * R, part], pot.at[i, R + X:XE, part], only=only))
            made[-1].start()
        corners.append(made)
        if i == 0:
            for r in rims:
                r.start()

    row = lax.broadcasted_iota(jnp.int32, (Y, Z), 0)
    lane = lax.broadcasted_iota(jnp.int32, (Y, Z), 1)
    valid_z = lane < Z - 1
    valid_y = (row < Y - 1) | gy["has_hi"]

    def forward(i):
        def along_x(k, carry):
            y0 = pl.multiple_of(k * 8, 8)
            p = [pot[i, j, pl.ds(y0, 8), :] for j in range(XE)]
            even, odd = filter_rows(p, X)
            for c in range(X):
                uv[c, pl.ds(y0, 8), 0:Z] = even[c]
                uv[c, pl.ds(y0, 8), Z:2 * Z] = odd[c]
            return carry

        lax.fori_loop(0, YE // 8, along_x, 0)

        def along_y(x, carry):
            hi, lo = split(uv[x])
            r = dot(wy[...], jnp.concatenate([hi, lo], 0))
            rows = pl.ds(pl.multiple_of(x * Y, Y), Y)
            for k, v in enumerate((r[0:Y, Z:], r[Y:, 0:Z], r[0:Y, 0:Z])):
                hi, lo = split(v)
                tri[k, rows, 0:Z] = hi
                tri[k, rows, Z:2 * Z] = lo
            return carry

        lax.fori_loop(0, X, along_y, 0, unroll=2)
        vx[i, 1:X + 1] = dot(tri[0], wz[0]).reshape(X, Y, Z)
        vyz[i, 0] = dot(tri[1], wz[0]).reshape(X, Y, Z)
        for x in range(X):
            stage_vy[i, 0, x:x + 1, :] = vyz[i, 0, x, 0:1, :]
            stage_vy[i, 1, x:x + 1, :] = vyz[i, 0, x, Y - 1:Y, :]
        made = [
            pair("gx", vx.at[i, X], vx.at[i, 0], vx.at[i, 1], vx.at[i, X + 1]),
            pair("gy", stage_vy.at[i, 1], rim_vy.at[i, 0], stage_vy.at[i, 0], rim_vy.at[i, 1]),
        ]
        for r in made:
            r.start()
        vyz[i, 1] = dot(tri[2], wz[1]).reshape(X, Y, Z)
        return made

    def keep(k, x, v):
        hi, lo = split(v)
        rows = pl.ds(pl.multiple_of(x * Y, Y), Y)
        tri[k, rows, 0:Z] = hi
        tri[k, rows, Z:2 * Z] = lo

    half = 0.5 * scale

    def faces_z(i):
        def step(x, carry):
            d, c, v = den[i, x], cot[i, x], vyz[i, 1, x]
            up = [pltpu.roll(t, Z - 1, 1) for t in (d, c, v)]
            lower, upper, bar = face_terms(d, up[0], c, up[1], v, up[2], valid_z)
            out[i, x] = c + (lower + pltpu.roll(upper, 1, 1))
            keep(2, x, half * (bar + pltpu.roll(bar, 1, 1)))
            return carry

        lax.fori_loop(0, X, step, 0)

    def faces_xy(i):
        first = face_terms(dcx[i, 0], dcx[i, 1], dcx[2 + i, 0], dcx[2 + i, 1], vx[i, 0], vx[i, 1], gx["has_lo"])

        def step(x, carry):
            upper_x, bar_x = carry
            d, c, v = dcx[i, x + 1], dcx[2 + i, x + 1], vx[i, x + 1]
            lower, upper, bar = face_terms(
                d, dcx[i, x + 2], c, dcx[2 + i, x + 2], v, vx[i, x + 2], (x < X - 1) | gx["has_hi"])
            total = lower + upper_x
            keep(0, x, half * (bar + bar_x))
            v = vyz[i, 0, x]
            one = pl.ds(x, 1)
            own = (d, c, v)
            below = (rim_y[0, i, one, :], rim_y[0, 2 + i, one, :], rim_vy[i, 0, one, :])
            above = (rim_y[1, i, one, :], rim_y[1, 2 + i, one, :], rim_vy[i, 1, one, :])
            up = [jnp.where(row == Y - 1, r, pltpu.roll(t, Y - 1, 0)) for t, r in zip(own, above)]
            ylower, yupper, ybar = face_terms(d, up[0], c, up[1], v, up[2], valid_y)
            _, eupper, ebar = face_terms(below[0], d[0:1], below[1], c[0:1], below[2], v[0:1], gy["has_lo"])
            total = total + ylower + jnp.where(row == 0, eupper, pltpu.roll(yupper, 1, 0))
            keep(1, x, half * (ybar + jnp.where(row == 0, ebar, pltpu.roll(ybar, 1, 0))))
            out[i, x] = out[i, x] + total
            return upper, bar

        lax.fori_loop(0, X, step, (first[1], first[2]))

    def backward(i):
        for k in range(3):
            zt[k] = dot(tri[k], wz[2 if k == 2 else 0]).reshape(X, Y, Z)

        def along_y(x, carry):
            va, vb, vc = (split(zt[k, x]) for k in range(3))
            blank = jnp.zeros((2 * Y, Z), BF16)
            rhs = jnp.concatenate([
                jnp.concatenate([vc[0], vc[1], vb[0], vb[1]], 0),
                jnp.concatenate([va[0], va[1], blank], 0)], 1)
            uv[x] = dot(wyt[...], rhs)
            return carry

        lax.fori_loop(0, X, along_y, 0, unroll=2)

        def along_x(k, carry):
            y0 = pl.multiple_of(k * 8, 8)
            q = [uv[c, pl.ds(y0, 8), 0:Z] for c in range(X)]
            p = [uv[c, pl.ds(y0, 8), Z:2 * Z] for c in range(X)]
            for j, v in enumerate(spread_rows(q, p)):
                spread[i, j, pl.ds(y0, 8), :] = v
            return carry

        lax.fori_loop(0, R // 8, along_x, 0)
        lax.fori_loop((R + Y) // 8, YE // 8, along_x, 0)
        made = []
        for part, only in ((slice(0, R), gy["has_lo"]), (slice(R + Y, YE), gy["has_hi"])):
            made.append(pair("gx", spread.at[i, R + X:XE, part], rx.at[i, 0, :, part],
                             spread.at[i, 0:R, part], rx.at[i, 1, :, part], only=only))
            made[-1].start()
        lax.fori_loop(R // 8, (R + Y) // 8, along_x, 0)
        centre = pair("gx", spread.at[i, R + X:XE, cy], rx.at[i, 0, :, cy],
                      spread.at[i, 0:R, cy], rx.at[i, 1, :, cy])
        centre.start()
        return made, centre

    def return_y(i, made):
        for m, part, has in ((made[0], slice(0, R), gy["has_lo"]), (made[1], slice(R + Y, YE), gy["has_hi"])):
            m.wait_recv()

            @pl.when(has)
            def _():
                spread[i, R:2 * R, part] = spread[i, R:2 * R, part] + rx[i, 0, :, part]
                spread[i, X:X + R, part] = spread[i, X:X + R, part] + rx[i, 1, :, part]
        back = pair("gy", spread.at[i, cx, R + Y:YE], ry.at[i, 0], spread.at[i, cx, 0:R], ry.at[i, 1])
        back.start()
        return back

    returned, centres, backs = [None, None], [None, None], [None, None]
    for i in range(2):
        to_x[i].wait_recv()
        for m in corners[i]:
            m.wait_recv()
        made = forward(i)
        faces_z(i)
        if i == 1:
            backs[0] = return_y(0, returned[0])
        if i == 0:
            for r in rims:
                r.wait_recv()
        for r in made:
            r.wait_recv()
        faces_xy(i)
        returned[i], centres[i] = backward(i)
    backs[1] = return_y(1, returned[1])
    for i in range(2):
        centres[i].wait_recv()
        spread[i, R:2 * R, cy] = spread[i, R:2 * R, cy] + rx[i, 0, :, cy]
        spread[i, X:X + R, cy] = spread[i, X:X + R, cy] + rx[i, 1, :, cy]
    for i in range(2):
        backs[i].wait_recv()
        spread[i, cx, R:2 * R] = spread[i, cx, R:2 * R] + ry[i, 0]
        spread[i, cx, Y:Y + R] = spread[i, cx, Y:Y + R] + ry[i, 1]

    def finish(x, carry):
        b = [spread[0, R + x, R:R + Y, :], spread[1, R + x, R:R + Y, :]]
        for i in range(2):
            out[i, x] = out[i, x] + (adh[0, i] * b[0] + adh[1, i] * b[1])
        return carry

    lax.fori_loop(0, X, finish, 0)
    for s in sends:
        s.wait_send()


def solution(mesh):
    nx, ny = mesh.shape["gx"], mesh.shape["gy"]

    def body(density, cotangent, adhesion):
        _, X, Y, Z = density.shape
        XE, YE = X + 2 * R, Y + 2 * R
        vmem = pl.BlockSpec(memory_space=pltpu.VMEM)
        return pl.pallas_call(
            lambda *refs: kernel(nx, ny, *refs),
            out_shape=jax.ShapeDtypeStruct(density.shape, F32),
            in_specs=[pl.BlockSpec(memory_space=pltpu.SMEM), vmem, vmem],
            out_specs=vmem,
            scratch_shapes=[
                pltpu.VMEM((2, XE, YE, Z), F32),
                pltpu.VMEM((X, YE, 2 * Z), F32),
                pltpu.VMEM((3, X * Y, 2 * Z), BF16),
                pltpu.VMEM((2, X + 2, Y, Z), F32),
                pltpu.VMEM((2, 2, X, Y, Z), F32),
                pltpu.VMEM((3, X, Y, Z), F32),
                pltpu.VMEM((4, X + 2, Y, Z), F32),
                pltpu.VMEM((2, 4, X, Z), F32),
                pltpu.VMEM((2, 4, X, Z), F32),
                pltpu.VMEM((2, 2, X, Z), F32),
                pltpu.VMEM((2, 2, X, Z), F32),
                pltpu.VMEM((2, XE, YE, Z), F32),
                pltpu.VMEM((2, 2, R, YE, Z), F32),
                pltpu.VMEM((2, 2, X, R, Z), F32),
                pltpu.VMEM((2 * Y, 2 * YE), BF16),
                pltpu.VMEM((YE, 4 * Y), BF16),
                pltpu.VMEM((3, 2 * Z, Z), BF16),
                pltpu.SemaphoreType.DMA((48,)),
                pltpu.SemaphoreType.DMA((48,)),
            ],
            compiler_params=pltpu.CompilerParams(
                collective_id=0, has_side_effects=True, vmem_limit_bytes=48 * 1024 * 1024
            ),
            cost_estimate=pl.CostEstimate(flops=10**9, bytes_accessed=3 * density.size * 4, transcendentals=0),
            name="adhesion_adjoint",
        )(adhesion, density, cotangent)

    spec = P(None, "gx", "gy", None)
    return jax.shard_map(body, mesh=mesh, in_specs=(spec, spec, P()), out_specs=spec, check_vma=False)
```

time: 154 us -> 53.7 us (0.35)
  waiting for transfers between devices: 83.1 us -> 0 us
  Pallas kernels: 0 us -> 49.7 us
  starting transfers between devices: 32 us -> 0 us
  matrix products: 17.6 us -> 0 us
  other arithmetic: 13.6 us -> 0 us
  local copies, waits for them, and re-layouts: 5.91 us -> 3.56 us
  between operations: 1.86 us -> 0.01 us
    ppermute x12 -> x0, waiting for transfers between devices: 83.1 us -> none  [the longest x6 47.2 us: padded(): lax.ppermute(tail, axis, [(i, (i + 1) % count) for i in range(ends)])]
    pallas_call x0 -> x1, Pallas kernels: none -> 49.7 us  [body(): pl.pallas_call(lambda *refs: kernel(nx, ny, *refs), out_shape=jax.ShapeDt...]
    ppermute x12 -> x0, starting transfers between devices: 32 us -> none  [the longest x6 22.1 us: padded(): lax.ppermute(tail, axis, [(i, (i + 1) % count) for i in range(ends)])]
    dot_general x16 -> x0, matrix products: 17.6 us -> none  [the longest x6 9.79 us: along_x(): return jnp.einsum('ck,fkyz->fcyz', matrix, values, precision=highest)]
    mul x8 -> x0, other arithmetic: 5.38 us -> none  [the longest x3 4.63 us: face_terms(): flux_bar * (0.5 * (lower_density + upper_density) - 0.5 * face_velocity /...]
    concatenate x6 -> x0, other arithmetic: 4.99 us -> none  [the longest x1 2.72 us: padded(): jnp.concatenate([lax.ppermute(tail, axis, [(i, (i + 1) % count) for i in...]
    unnamed x14 -> x7, local copies, waits for them, and re-layouts: 0.65 us -> 3.56 us
    slice x7 -> x0, local copies, waits for them, and re-layouts: 2.88 us -> none  [the longest x1 0.98 us: body(): velocity_z = along_x(even_x, widened_x[4:6])]
  transfers between devices with their start and end apart: 12 -> 0, of which waited for: 8 -> 0; matrix products, arithmetic and copies ran while one was open for 7% -> 0% of each run, Pallas kernels for 0% -> 0%
where the time goes in v1:
time: 53.7 us; the launch traced here: 53.3 us
  Pallas kernels  49.7 us (93%)
  local copies, waits for them, and re-layouts  3.56 us (7%)
    pallas_call x1, Pallas kernels, body(): pl.pallas_call(lambda *refs: kernel(nx, ny, *refs), out_shape=jax.ShapeDt...  49.7 us
    unnamed x7, local copies, waits for them, and re-layouts  3.56 us

profile of v1, /device:TPU:17, one launch (start us, length us, event | category | flops | bytes accessed | tf_op | source)
XLA Modules:
  0.0 53.3 jit_solution(14171648199527777352)
XLA Ops:
  0.0 0.0 copy-start
  0.0 1.0 %copy-done = f32[2,16,32,128]{3,2,1,0:T(8,128)S(1)} copy-done((f32[2,16,32,128]{3,2,1,0:T(8,128)S(1)}, f32[2,16,32,128]{3,2,1,0:T(8,128)}, u32[]{:S(2)}) %copy-start) | copy-done | bytes 524312
  1.0 0.0 copy-start.1
  1.0 1.0 %copy-done.1 = f32[2,16,32,128]{3,2,1,0:T(8,128)S(1)} copy-done((f32[2,16,32,128]{3,2,1,0:T(8,128)S(1)}, f32[2,16,32,128]{3,2,1,0:T(8,128)}, u32[]{:S(2)}) %copy-start.1) | copy-done | bytes 524312
  2.1 0.0 copy-start.2
  2.1 0.7 %copy-done.2 = f32[2,2]{1,0:T(2,128)S(1)} copy-done((f32[2,2]{1,0:T(2,128)S(1)}, f32[2,2]{1,0:T(2,128)}, u32[]{:S(2)}) %copy-start.2) | copy-done | bytes 40
  2.8 49.7 %adhesion_adjoint.1 = f32[2,16,32,128]{3,2,1,0:T(8,128)S(1)} custom-call(f32[2,2]{1,0:T(2,128)S(1)} %copy-done.2, f32[2,16,32,128]{3,2,1,0:T(8,128)S(1)} %copy-done, f32[2,16,32,128]{3,2,1,0:T(8,128)S(1)} %copy-done.1), custom_call_target="tpu_custom_call" | custom-call | flops 1000000000 | bytes 1572864 | tf_op jit(solution)/shard_map/adhesion_adjoint/pallas_call | solution.py:474
  52.5 0.8 %copy.5 = f32[2,16,32,128]{3,2,1,0:T(8,128)} copy(f32[2,16,32,128]{3,2,1,0:T(8,128)S(1)} %adhesion_adjoint.1) | data formatting | bytes 1048576
Async XLA Ops:
  0.0 1.0 %copy-start = (f32[2,16,32,128]{3,2,1,0:T(8,128)S(1)}, f32[2,16,32,128]{3,2,1,0:T(8,128)}, u32[]{:S(2)}) copy-start(f32[2,16,32,128]{3,2,1,0:T(8,128)} %refs_1_.1) | copy-start | bytes 1572868
  1.0 1.0 %copy-start.1 = (f32[2,16,32,128]{3,2,1,0:T(8,128)S(1)}, f32[2,16,32,128]{3,2,1,0:T(8,128)}, u32[]{:S(2)}) copy-start(f32[2,16,32,128]{3,2,1,0:T(8,128)} %refs_2_.1) | copy-start | bytes 1572868
  2.1 0.7 %copy-start.2 = (f32[2,2]{1,0:T(2,128)S(1)}, f32[2,2]{1,0:T(2,128)}, u32[]{:S(2)}) copy-start(f32[2,2]{1,0:T(2,128)} %refs_0_.1) | copy-start | bytes 52

commit v2 on v1

--- a/solution.py
+++ b/solution.py
@@ -259,12 +259,13 @@
                          pot.at[i, cx, R:2 * R], pot.at[i, cx, R + Y:YE]))
         to_x.append(pair("gx", pot.at[i, X:X + R, cy], pot.at[i, 0:R, cy],
                          pot.at[i, R:2 * R, cy], pot.at[i, R + X:XE, cy]))
-        to_y[i].start()
-        to_x[i].start()
     rims = [
         pair("gx", dcx.at[:, X], dcx.at[:, 0], dcx.at[:, 1], dcx.at[:, X + 1]),
         pair("gy", stage_y.at[1], rim_y.at[0], stage_y.at[0], rim_y.at[1]),
     ]
+
+    to_y[0].start()
+    to_x[0].start()
 
     o = offsets(Y, YE, R)
     for k in range(2):
@@ -280,18 +281,19 @@
         wz[1, k * Z:(k + 1) * Z, :] = odd_int(-o).astype(BF16)
         wz[2, k * Z:(k + 1) * Z, :] = odd_int(o).astype(BF16)
 
-    corners = []
-    for i in range(2):
+    def send_corners(i):
         to_y[i].wait_recv()
         made = []
         for part, only in ((slice(0, R), gy["has_lo"]), (slice(R + Y, YE), gy["has_hi"])):
             made.append(pair("gx", pot.at[i, X:X + R, part], pot.at[i, 0:R, part],
                              pot.at[i, R:2 * R, part], pot.at[i, R + X:XE, part], only=only))
             made[-1].start()
-        corners.append(made)
-        if i == 0:
-            for r in rims:
-                r.start()
+        return made
+
+    corners = [send_corners(0), None]
+    to_y[1].start()
+    for r in rims:
+        r.start()
 
     row = lax.broadcasted_iota(jnp.int32, (Y, Z), 0)
     lane = lax.broadcasted_iota(jnp.int32, (Y, Z), 1)
@@ -412,7 +414,6 @@
         lax.fori_loop(R // 8, (R + Y) // 8, along_x, 0)
         centre = pair("gx", spread.at[i, R + X:XE, cy], rx.at[i, 0, :, cy],
                       spread.at[i, 0:R, cy], rx.at[i, 1, :, cy])
-        centre.start()
         return made, centre
 
     def return_y(i, made):
@@ -432,11 +433,15 @@
         to_x[i].wait_recv()
         for m in corners[i]:
             m.wait_recv()
+        if i == 0:
+            to_x[1].start()
         made = forward(i)
         faces_z(i)
         if i == 1:
             backs[0] = return_y(0, returned[0])
+            centres[0].start()
         if i == 0:
+            corners[1] = send_corners(1)
             for r in rims:
                 r.wait_recv()
         for r in made:
@@ -444,6 +449,7 @@
         faces_xy(i)
         returned[i], centres[i] = backward(i)
     backs[1] = return_y(1, returned[1])
+    centres[1].start()
     for i in range(2):
         centres[i].wait_recv()
         spread[i, R:2 * R, cy] = spread[i, R:2 * R, cy] + rx[i, 0, :, cy]

time: 53.7 us -> 51.8 us (0.965)
  Pallas kernels: 49.7 us -> 48 us
    pallas_call x1, Pallas kernels: 49.7 us -> 48 us  [body(): pl.pallas_call(lambda *refs: kernel(nx, ny, *refs), out_shape=jax.ShapeDt...]
where the time goes in v2:
time: 51.8 us; the launch traced here: 51.6 us
  Pallas kernels  48 us (93%)
  local copies, waits for them, and re-layouts  3.56 us (7%)
    pallas_call x1, Pallas kernels, body(): pl.pallas_call(lambda *refs: kernel(nx, ny, *refs), out_shape=jax.ShapeDt...  48 us
    unnamed x7, local copies, waits for them, and re-layouts  3.56 us

profile of v2, /device:TPU:17, one launch (start us, length us, event | category | flops | bytes accessed | tf_op | source)
XLA Modules:
  0.0 51.6 jit_solution(14532013393631795844)
XLA Ops:
  0.0 0.0 copy-start
  0.0 1.0 %copy-done = f32[2,16,32,128]{3,2,1,0:T(8,128)S(1)} copy-done((f32[2,16,32,128]{3,2,1,0:T(8,128)S(1)}, f32[2,16,32,128]{3,2,1,0:T(8,128)}, u32[]{:S(2)}) %copy-start) | copy-done | bytes 524312
  1.0 0.0 copy-start.1
  1.0 1.0 %copy-done.1 = f32[2,16,32,128]{3,2,1,0:T(8,128)S(1)} copy-done((f32[2,16,32,128]{3,2,1,0:T(8,128)S(1)}, f32[2,16,32,128]{3,2,1,0:T(8,128)}, u32[]{:S(2)}) %copy-start.1) | copy-done | bytes 524312
  2.1 0.0 copy-start.2
  2.1 0.7 %copy-done.2 = f32[2,2]{1,0:T(2,128)S(1)} copy-done((f32[2,2]{1,0:T(2,128)S(1)}, f32[2,2]{1,0:T(2,128)}, u32[]{:S(2)}) %copy-start.2) | copy-done | bytes 40
  2.8 48.0 %adhesion_adjoint.1 = f32[2,16,32,128]{3,2,1,0:T(8,128)S(1)} custom-call(f32[2,2]{1,0:T(2,128)S(1)} %copy-done.2, f32[2,16,32,128]{3,2,1,0:T(8,128)S(1)} %copy-done, f32[2,16,32,128]{3,2,1,0:T(8,128)S(1)} %copy-done.1), custom_call_target="tpu_custom_call" | custom-call | flops 1000000000 | bytes 1572864 | tf_op jit(solution)/shard_map/adhesion_adjoint/pallas_call | solution.py:480
  50.8 0.8 %copy.5 = f32[2,16,32,128]{3,2,1,0:T(8,128)} copy(f32[2,16,32,128]{3,2,1,0:T(8,128)S(1)} %adhesion_adjoint.1) | data formatting | bytes 1048576
Async XLA Ops:
  0.0 1.0 %copy-start = (f32[2,16,32,128]{3,2,1,0:T(8,128)S(1)}, f32[2,16,32,128]{3,2,1,0:T(8,128)}, u32[]{:S(2)}) copy-start(f32[2,16,32,128]{3,2,1,0:T(8,128)} %refs_1_.1) | copy-start | bytes 1572868
  1.0 1.0 %copy-start.1 = (f32[2,16,32,128]{3,2,1,0:T(8,128)S(1)}, f32[2,16,32,128]{3,2,1,0:T(8,128)}, u32[]{:S(2)}) copy-start(f32[2,16,32,128]{3,2,1,0:T(8,128)} %refs_2_.1) | copy-start | bytes 1572868
  2.1 0.7 %copy-start.2 = (f32[2,2]{1,0:T(2,128)S(1)}, f32[2,2]{1,0:T(2,128)}, u32[]{:S(2)}) copy-start(f32[2,2]{1,0:T(2,128)} %refs_0_.1) | copy-start | bytes 52
